TPU v7x, 256 devices: a whole 4x4x8 slice. The times are simulated.
256 devices in a mesh: ctx: 32 (over y, z_lo, core), rep: 8 (over z_hi, x).
Axes of the slice: x: 4, y: 4, z: 8 (z_hi: 2, z_lo: 4; z = z_hi * 4 + z_lo), core: 2. Of those that a mesh axis runs over, the one named last changes fastest.
Arguments:
- hidden: bfloat16 [8, 4096, 8192], P('rep', 'ctx'), may hold values from -6 to 6
- queries: bfloat16 [8, 4096, 4096], P('rep', 'ctx'), may hold values from -128 to 128
- keys: bfloat16 [8, 4096, 512], P('rep', 'ctx'), may hold values from -6 to 6
- values: bfloat16 [8, 4096, 512], P('rep', 'ctx'), may hold values from -6 to 6
- out_grad: bfloat16 [8, 4096, 4096], P('rep', 'ctx'), may hold values from -6 to 6
- positions: int32 [8, 4096], P('rep', 'ctx'), may hold values from 0 to 1023, as said below
Outputs:
- query_grad: bfloat16 [8, 4096, 4096], P('rep', 'ctx')
- weight_gradient: float32 [8192, 1024], P('ctx', 'rep')
Inputs may be any that keep to these rules, and one draw needn't show every extreme that they name: Within a replica's row each position is 0 (a document starts) or one more than the position before it; the first token's position may exceed 0, its document having begun before the stretch; no document of the stretch spans more than 1024 positions.
All inputs are finite; a program needn't handle non-finite values.
Results may differ from a plain program's by a relative error of at most 0.014.
Values may be sent and summed in bfloat16 or wider, within the bound.
A program may use at most 128 MiB of HBM per device.

v0:
```python
import math

import jax
import jax.numpy as jnp
from jax import lax
from jax.sharding import PartitionSpec as P

QUERY_HEADS = 32
KEY_VALUE_HEADS = 4
HEAD_SIZE = 128


def attend(query_heads, grad_heads, key_head_gradient, value_head_gradient, places):
    total = query_heads.shape[0]
    block = min(512, total)
    reach = total // 4
    span = min(total, block + reach)
    scale = HEAD_SIZE ** (-0.5)

    def one_block(carry, block_index):
        key_acc, value_acc = carry
        first_query = block_index * block
        first_key = jnp.clip(first_query - reach, 0, total - span)
        query_block = lax.dynamic_slice_in_dim(query_heads, first_query, block, 0)
        grad_block = lax.dynamic_slice_in_dim(grad_heads, first_query, block, 0)
        key_window = lax.dynamic_slice_in_dim(key_head_gradient, first_key, span, 0)
        value_window = lax.dynamic_slice_in_dim(value_head_gradient, first_key, span, 0)
        place_block = lax.dynamic_slice_in_dim(places, first_query, block, 0)
        scores = (
            jnp.einsum("qhd,khd->hqk", query_block, key_window, preferred_element_type=jnp.float32)
            * scale
        )
        query_index = first_query + jnp.arange(block, dtype=jnp.int32)
        key_index = first_key + jnp.arange(span, dtype=jnp.int32)
        visible = (key_index[None, :] <= query_index[:, None]) & (
            key_index[None, :] >= (query_index - place_block)[:, None]
        )
        masked = jnp.where(visible[None], scores, -1e30)
        highest = jnp.max(masked, axis=-1, keepdims=True)
        raised = jnp.where(visible[None], jnp.exp(masked - highest), 0.0)
        probs = raised / jnp.sum(raised, axis=-1, keepdims=True)
        weights = probs.astype(jnp.bfloat16)
        attended = jnp.einsum(
            "hqk,khd->qhd", weights, value_window, preferred_element_type=jnp.float32
        )
        delta = jnp.sum(grad_block.astype(jnp.float32) * attended, axis=-1)
        dprob = jnp.einsum(
            "qhd,khd->hqk", grad_block, value_window, preferred_element_type=jnp.float32
        )
        dscore = (probs * (dprob - delta.T[:, :, None]) * scale).astype(jnp.bfloat16)
        query_grad = jnp.einsum(
            "hqk,khd->qhd", dscore, key_window, preferred_element_type=jnp.float32
        ).astype(jnp.bfloat16)
        key_part = jnp.einsum(
            "hqk,qhd->khd", dscore, query_block, preferred_element_type=jnp.float32
        )
        value_part = jnp.einsum(
            "hqk,qhd->khd", weights, grad_block, preferred_element_type=jnp.float32
        )
        key_acc = lax.dynamic_update_slice_in_dim(
            key_acc, lax.dynamic_slice_in_dim(key_acc, first_key, span, 0) + key_part, first_key, 0
        )
        value_acc = lax.dynamic_update_slice_in_dim(
            value_acc,
            lax.dynamic_slice_in_dim(value_acc, first_key, span, 0) + value_part,
            first_key,
            0,
        )
        return ((key_acc, value_acc), query_grad)

    zero_start = jnp.zeros(key_head_gradient.shape, jnp.float32)
    (key_acc, value_acc), query_grads = lax.scan(
        one_block, (zero_start, zero_start), jnp.arange(total // block, dtype=jnp.int32)
    )
    return (
        query_grads.reshape(query_heads.shape),
        key_acc.astype(jnp.bfloat16),
        value_acc.astype(jnp.bfloat16),
    )


def body(hidden, queries, keys, values, out_grad, positions):
    replica_rows = queries.shape[1]
    group_count = QUERY_HEADS // KEY_VALUE_HEADS
    query_rows = queries[0].reshape(replica_rows, QUERY_HEADS, HEAD_SIZE)
    grad_rows = out_grad[0].reshape(replica_rows, QUERY_HEADS, HEAD_SIZE)
    places = lax.all_gather(positions, "ctx", axis=1, tiled=True)[0]
    device_count = lax.axis_size("ctx")
    own_heads = QUERY_HEADS // device_count
    key_copies = jnp.broadcast_to(
        keys[0].reshape(replica_rows, KEY_VALUE_HEADS, 1, HEAD_SIZE),
        (replica_rows, KEY_VALUE_HEADS, group_count, HEAD_SIZE),
    ).reshape(replica_rows, device_count, own_heads, HEAD_SIZE)
    value_copies = jnp.broadcast_to(
        values[0].reshape(replica_rows, KEY_VALUE_HEADS, 1, HEAD_SIZE),
        (replica_rows, KEY_VALUE_HEADS, group_count, HEAD_SIZE),
    ).reshape(replica_rows, device_count, own_heads, HEAD_SIZE)
    query_split = query_rows.reshape(replica_rows, device_count, own_heads, HEAD_SIZE)
    grad_split = grad_rows.reshape(replica_rows, device_count, own_heads, HEAD_SIZE)
    parts = (
        lax.all_to_all(query_split, "ctx", split_axis=1, concat_axis=0, tiled=True),
        lax.all_to_all(grad_split, "ctx", split_axis=1, concat_axis=0, tiled=True),
        lax.all_to_all(key_copies, "ctx", split_axis=1, concat_axis=0, tiled=True),
        lax.all_to_all(value_copies, "ctx", split_axis=1, concat_axis=0, tiled=True),
    )
    every_row = parts[0].shape[0]
    some_heads = parts[0].shape[2]
    flat = [piece.reshape(every_row, some_heads, HEAD_SIZE) for piece in parts]
    results = attend(flat[0], flat[1], flat[2], flat[3], places)
    query_four, key_four, value_four = tuple(
        (result.reshape(every_row, 1, some_heads, HEAD_SIZE) for result in results)
    )
    every_row = query_four.shape[0]
    head_query = query_four.reshape(every_row, own_heads, HEAD_SIZE)
    key_per_head = key_four.reshape(every_row, own_heads, HEAD_SIZE)
    value_per_head = value_four.reshape(every_row, own_heads, HEAD_SIZE)
    back_query, back_key, back_value = (
        lax.all_to_all(head_query, "ctx", split_axis=0, concat_axis=1, tiled=True),
        lax.all_to_all(key_per_head, "ctx", split_axis=0, concat_axis=1, tiled=True),
        lax.all_to_all(value_per_head, "ctx", split_axis=0, concat_axis=1, tiled=True),
    )
    query_out = back_query.reshape(1, replica_rows, QUERY_HEADS * HEAD_SIZE)
    key_total = (
        back_key.astype(jnp.float32)
        .reshape(replica_rows, KEY_VALUE_HEADS, group_count, HEAD_SIZE)
        .sum(axis=2)
        .astype(jnp.bfloat16)
    )
    value_total = (
        back_value.astype(jnp.float32)
        .reshape(replica_rows, KEY_VALUE_HEADS, group_count, HEAD_SIZE)
        .sum(axis=2)
        .astype(jnp.bfloat16)
    )
    key_value_gradients = jnp.concatenate(
        [
            key_total.reshape(replica_rows, KEY_VALUE_HEADS * HEAD_SIZE),
            value_total.reshape(replica_rows, KEY_VALUE_HEADS * HEAD_SIZE),
        ],
        axis=1,
    )
    token_rows = hidden[0]
    row_slices = lax.all_to_all(token_rows, "ctx", split_axis=1, concat_axis=0, tiled=True)
    grads_all = lax.all_gather(key_value_gradients, "ctx", axis=0, tiled=True)
    run_count = lax.axis_size("ctx")
    per_turn = math.gcd(run_count, 4)
    own_rows = row_slices.shape[1]
    columns = grads_all.shape[1]
    hidden_sequences = row_slices.reshape(run_count // per_turn, per_turn, replica_rows, own_rows)
    gradient_runs = grads_all.reshape(run_count // per_turn, per_turn, replica_rows, columns)

    def add_runs(total, pair):
        terms = jnp.einsum(
            "gtd,gtc->gdc", pair[0], pair[1], preferred_element_type=jnp.float32
        ).astype(jnp.bfloat16)
        return (total + jnp.sum(terms.astype(jnp.float32), axis=0), None)

    row_sum, unused_slot = lax.scan(
        add_runs, jnp.zeros((own_rows, columns), jnp.float32), (hidden_sequences, gradient_runs)
    )
    weight_tile = lax.psum_scatter(row_sum, "rep", scatter_dimension=1, tiled=True)
    return (query_out, weight_tile)


def solution(mesh):
    in_specs = (
        P("rep", "ctx", None),
        P("rep", "ctx", None),
        P("rep", "ctx", None),
        P("rep", "ctx", None),
        P("rep", "ctx", None),
        P("rep", "ctx"),
    )
    out_specs = (P("rep", "ctx", None), P("ctx", "rep"))
    return jax.shard_map(body, mesh=mesh, in_specs=in_specs, out_specs=out_specs, check_vma=False)
```

profile of v0, /device:TPU:6, one launch (start us, length us, event | category | flops | bytes accessed | tf_op | source)
XLA Modules:
  0.0 730.6 jit_solution(17737223887054672629)
XLA Ops:
  9.5 9.1 %all-to-all-start = ((bf16[128,32,1,128]{0,3,2,1:T(8,128)(2,1)}), bf16[128,32,1,128]{0,3,2,1:T(8,128)(2,1)S(1)}, u32[]{:S(2)}, u32[]{:S(2)}) async-start(bf16[128,32,1,128]{0,3,2,1:T(8,128)(2,1)} %bitcast.15), calls=%async_computation | async-start | bytes 2097152 | tf_op jit(solution)/shard_map/all_to_all | solution.py:101
  19.9 26.6 %all-to-all-done = bf16[128,32,1,128]{0,3,2,1:T(8,128)(2,1)S(1)} async-done(((bf16[128,32,1,128]{0,3,2,1:T(8,128)(2,1)}), bf16[128,32,1,128]{0,3,2,1:T(8,128)(2,1)S(1)}, u32[]{:S(2)}, u32[]{:S(2)}) %all-to-all-start) | async-done | bytes 1048608 | tf_op jit(solution)/shard_map/all_to_all | solution.py:101
  46.5 3.9 all-to-all-start.2
  50.6 27.9 %all-to-all-done.2 = bf16[128,32,1,128]{0,3,2,1:T(8,128)(2,1)S(1)} async-done(((bf16[128,32,1,128]{0,3,2,1:T(8,128)(2,1)}), bf16[128,32,1,128]{0,3,2,1:T(8,128)(2,1)S(1)}, u32[]{:S(2)}, u32[]{:S(2)}) %all-to-all-start.2) | async-done | bytes 1048608 | tf_op jit(solution)/shard_map/all_to_all | solution.py:102
  79.6 4.8 all-to-all-start.1
  84.5 27.9 %all-to-all-done.1 = bf16[128,32,1,128]{3,0,2,1:T(8,128)(2,1)} async-done(((bf16[128,32,1,128]{3,0,2,1:T(8,128)(2,1)}), bf16[128,32,1,128]{3,0,2,1:T(8,128)(2,1)}, u32[]{:S(2)}, u32[]{:S(2)}) %all-to-all-start.1) | async-done | bytes 1048608 | tf_op jit(solution)/shard_map/all_to_all | solution.py:103
  113.6 4.7 all-to-all-start.3
  118.3 55.8 %all_gather.6 = s32[1,4096]{1,0:T(1,128)S(1)} all-gather(s32[1,128]{1,0:T(1,128)S(1)} %copy-done.8), channel_id=1, replica_groups=mesh['ctx'=32,'rep'=8] {'ctx'}, dimensions={1}, use_global_device_ids=true | all-gather | bytes 16896 | tf_op jit(solution)/shard_map/all_gather | solution.py:87
  180.4 233.3 %while.27 = (s32[]{:T(128)}, f32[4096,1,128]{0,2,1:T(8,128)}, f32[4096,1,128]{0,2,1:T(8,128)}, bf16[8,512,1,128]{3,1,0,2:T(8,128)(2,1)}, s32[8]{0:T(128)}, /*ind...) while((s32[]{:T(128)}, f32[4096,1,128]{0,2,1:T(8,128)}, ...), condition=%wide.region_4.5_spmd, body=%wide.region_0.4_spmd.sunk | while | flops 1227490304 | bytes 42787656 | solution.py:72
  192.1 2.6 fusion.75
  194.7 4.8 dynamic_update_slice.24
  202.5 2.4 fusion.76
  205.0 4.8 dynamic_update_slice.25
  221.5 2.6 fusion.75
  224.1 4.8 dynamic_update_slice.24
  234.3 4.8 dynamic_update_slice.25
  250.9 2.6 fusion.75
  253.5 4.8 dynamic_update_slice.24
  263.7 4.8 dynamic_update_slice.25
  280.3 2.6 fusion.75
  282.9 4.8 dynamic_update_slice.24
  290.7 2.4 fusion.76
  293.2 4.8 dynamic_update_slice.25
  309.7 2.6 fusion.75
  312.3 4.8 dynamic_update_slice.24
  322.6 4.8 dynamic_update_slice.25
  339.1 2.6 fusion.75
  341.7 4.7 dynamic_update_slice.24
  349.4 2.4 fusion.76
  351.9 4.8 dynamic_update_slice.25
  368.4 2.6 fusion.75
  370.9 4.6 dynamic_update_slice.24
  381.0 4.6 dynamic_update_slice.25
  397.4 2.5 fusion.75
  399.9 4.2 dynamic_update_slice.24
  409.5 4.2 dynamic_update_slice.25
  420.9 4.8 all-to-all-start.6
  429.1 24.4 %all-to-all-done.6 = bf16[32,2,8192]{2,1,0:T(2,128)(2,1)} async-done(((bf16[32,2,8192]{2,1,0:T(2,128)(2,1)}), bf16[32,2,8192]{2,1,0:T(2,128)(2,1)}, u32[]{:S(2)}, u32[]{:S(2)}) %all-to-all-start.6) | async-done | bytes 1048608 | tf_op jit(solution)/shard_map/all_to_all | solution.py:119
  453.5 3.9 all-to-all-start.7
  457.5 4.3 reshape.171
  464.5 20.9 %all-to-all-done.7 = bf16[32,2,8192]{2,1,0:T(2,128)(2,1)S(1)} async-done(((bf16[32,2,8192]{2,1,0:T(2,128)(2,1)}), bf16[32,2,8192]{2,1,0:T(2,128)(2,1)S(1)}, u32[]{:S(2)}, u32[]{:S(2)}) %all-to-all-start.7) | async-done | bytes 1048608 | tf_op jit(solution)/shard_map/all_to_all | solution.py:120
  488.3 2.5 copy.62
  490.8 4.8 all-to-all-start.5
  495.6 108.9 %all-gather.2.cloned.1.call-done = bf16[4096,1024]{0,1:T(8,128)(2,1)} async-done(((bf16[128,1024]{0,1:T(8,128)(2,1)}), bf16[4096,1024]{0,1:T(8,128)(2,1)}) %all-gather.2.cloned.1.call-update) | async-done | bytes 8388624 | tf_op jit(solution)/shard_map/all_gather | solution.py:144
  604.5 12.0 %copy.63 = bf16[4096,1024]{1,0:T(8,128)(2,1)} copy(bf16[4096,1024]{0,1:T(8,128)(2,1)} %all-gather.2.cloned.1.call-done) | data formatting | bytes 16777216
  616.5 19.8 %while.28 = (s32[]{:T(128)}, f32[256,1024]{1,0:T(8,128)S(1)}, bf16[8,4,128,256]{2,3,1,0:T(8,128)(2,1)}, bf16[8,4,128,1024]{3,2,1,0:T(8,128)(2,1)}, s32[]{:T(128)}, /*index=5*/s32[]{:T(128)}) while((s32[]{:T(128)}, f32[256,1024]{1,0:T(8,128)S(1)}, bf16[8,4,128,256]{2,3,1,0:T(8,128)(2,1)}, bf16[8,4,128,1024]{3,2,1,0:T(8,128)(2,1)}, ...), condition=%wide.region_9.10_spmd.clone, body=%wide.region_7.9_spmd.clone.sunk | while | flops 271843328 | bytes 5506127 | solution.py:158
  639.0 39.5 %all_to_all.109 = bf16[32,2,8192]{2,1,0:T(2,128)(2,1)S(1)} all-to-all(bf16[32,2,8192]{2,1,0:T(2,128)(2,1)S(1)} %reshape.166), channel_id=1, replica_groups=mesh['ctx'=32,'rep'=8] {'ctx'}, dimensions={0} | all-to-all | bytes 2097152 | tf_op jit(solution)/shard_map/all_to_all | solution.py:118
  681.7 42.1 %reduce-scatter.2.cloned.1.call-done = f32[256,128]{1,0:T(8,128)} async-done(((f32[256,1024]{1,0:T(8,128)}), f32[256,128]{1,0:T(8,128)}) %reduce-scatter.2.cloned.1.call-update) | async-done | bytes 131088 | tf_op jit(solution)/shard_map/reduce_scatter | solution.py:161
  (201 shorter events, 178.3 us)
Async XLA Ops:
  7.2 11.4 %copy-start.5 = (bf16[1,128,4096]{2,1,0:T(8,128)(2,1)S(1)}, bf16[1,128,4096]{2,1,0:T(8,128)(2,1)}, u32[]{:S(2)}) copy-start(bf16[1,128,4096]{2,1,0:T(8,128)(2,1)} %param.14) | copy-start | bytes 3145732
  9.5 41.0 %copy-start.6 = (bf16[1,128,512]{2,1,0:T(8,128)(2,1)S(1)}, bf16[1,128,512]{2,1,0:T(8,128)(2,1)}, u32[]{:S(2)}) copy-start(bf16[1,128,512]{2,1,0:T(8,128)(2,1)} %param.12) | copy-start | bytes 393220
  9.5 37.0 %all-to-all-start = ((bf16[128,32,1,128]{0,3,2,1:T(8,128)(2,1)}), bf16[128,32,1,128]{0,3,2,1:T(8,128)(2,1)S(1)}, u32[]{:S(2)}, u32[]{:S(2)}) async-start(bf16[128,32,1,128]{0,3,2,1:T(8,128)(2,1)} %bitcast.15), calls=%async_computation | async-start | bytes 2097152 | tf_op jit(solution)/shard_map/all_to_all | solution.py:101
  19.9 64.6 %copy-start.7 = (bf16[1,128,512]{2,1,0:T(8,128)(2,1)S(1)}, bf16[1,128,512]{2,1,0:T(8,128)(2,1)}, u32[]{:S(2)}) copy-start(bf16[1,128,512]{2,1,0:T(8,128)(2,1)} %param.13) | copy-start | bytes 393220
  46.5 31.9 %all-to-all-start.2 = ((bf16[128,32,1,128]{0,3,2,1:T(8,128)(2,1)}), bf16[128,32,1,128]{0,3,2,1:T(8,128)(2,1)S(1)}, u32[]{:S(2)}, u32[]{:S(2)}) async-start(bf16[128,32,1,128]{0,3,2,1:T(8,128)(2,1)} %bitcast.24), calls=%async_computation.2 | async-start | bytes 2097152 | tf_op jit(solution)/shard_map/all_to_all | solution.py:102
  79.6 38.6 %copy-start.8 = (s32[1,128]{1,0:T(1,128)S(1)}, s32[1,128]{1,0:T(1,128)}, u32[]{:S(2)}) copy-start(s32[1,128]{1,0:T(1,128)} %param.15) | copy-start | bytes 1540
  79.6 32.7 %all-to-all-start.1 = ((bf16[128,32,1,128]{3,0,2,1:T(8,128)(2,1)}), bf16[128,32,1,128]{3,0,2,1:T(8,128)(2,1)}, u32[]{:S(2)}, u32[]{:S(2)}) async-start(bf16[128,32,1,128]{3,0,2,1:T(8,128)(2,1)} %bitcast.20), calls=%async_computation.1 | async-start | bytes 2097152 | tf_op jit(solution)/shard_map/all_to_all | solution.py:103
  113.6 63.2 %all-to-all-start.3 = ((bf16[128,32,1,128]{3,0,2,1:T(8,128)(2,1)}), bf16[128,32,1,128]{3,0,2,1:T(8,128)(2,1)}, u32[]{:S(2)}, u32[]{:S(2)}) async-start(bf16[128,32,1,128]{3,0,2,1:T(8,128)(2,1)} %bitcast.28), calls=%async_computation.3 | async-start | bytes 2097152 | tf_op jit(solution)/shard_map/all_to_all | solution.py:104
  190.9 1.2 copy-start
  220.3 1.2 copy-start
  249.7 1.2 copy-start
  279.1 1.2 copy-start
  308.5 1.2 copy-start
  337.9 1.2 copy-start
  367.2 1.2 copy-start
  396.2 1.2 copy-start
  417.4 8.3 %copy-start.2 = (f32[4096,1,128]{0,2,1:T(8,128)S(1)}, f32[4096,1,128]{0,2,1:T(8,128)}, u32[]{:S(2)}) copy-start(f32[4096,1,128]{0,2,1:T(8,128)} %get-tuple-element.153) | copy-start | bytes 6291460
  420.9 32.6 %all-to-all-start.6 = ((bf16[32,2,8192]{2,1,0:T(2,128)(2,1)}), bf16[32,2,8192]{2,1,0:T(2,128)(2,1)}, u32[]{:S(2)}, u32[]{:S(2)}) async-start(bf16[32,2,8192]{2,1,0:T(2,128)(2,1)} %reshape.170), calls=%async_computation.6 | async-start | bytes 2097152 | tf_op jit(solution)/shard_map/all_to_all | solution.py:119
  453.5 31.9 %all-to-all-start.7 = ((bf16[32,2,8192]{2,1,0:T(2,128)(2,1)}), bf16[32,2,8192]{2,1,0:T(2,128)(2,1)S(1)}, u32[]{:S(2)}, u32[]{:S(2)}) async-start(bf16[32,2,8192]{2,1,0:T(2,128)(2,1)} %reshape.168), calls=%async_computation.7 | async-start | bytes 2097152 | tf_op jit(solution)/shard_map/all_to_all | solution.py:120
  457.5 147.0 %all-gather.2.cloned.1.call-start = ((), (), s32[]{:S(2)}) async-start(), calls=%async_computation.9 | async-start | bytes 8650752 | tf_op jit(solution)/shard_map/all_gather | solution.py:144
  486.6 1.7 copy-start.3
  490.8 125.7 %all-to-all-start.5 = ((bf16[128,32,256]{0,2,1:T(8,128)(2,1)}), bf16[128,32,256]{0,2,1:T(8,128)(2,1)}, u32[]{:S(2)}, u32[]{:S(2)}) async-start(bf16[128,32,256]{0,2,1:T(8,128)(2,1)} %bitcast.35), calls=%async_computation.5 | async-start | bytes 4194304 | tf_op jit(solution)/shard_map/all_to_all | solution.py:143
  495.5 228.2 %reduce-scatter.2.cloned.1.call-start = ((), (), s32[]{:S(2)}) async-start(), calls=%async_computation.10 | async-start | bytes 1179648 | tf_op jit(solution)/shard_map/reduce_scatter | solution.py:161
  616.5 20.8 %copy-start.4 = (bf16[8,512,1,128]{3,1,0,2:T(8,128)(2,1)S(1)}, bf16[8,512,1,128]{3,1,0,2:T(8,128)(2,1)}, u32[]{:S(2)}) copy-start(bf16[8,512,1,128]{3,1,0,2:T(8,128)(2,1)} %get-tuple-element.151) | copy-start | bytes 3145732
  636.3 1.0 copy-start.1
Sparse Core Ops, SparseCore 0:
  487.8 116.6 all-gather.1
  637.4 86.3 reduce-scatter.1
where the time goes:
time: 736 us; the launch traced here: 731 us
  waiting for transfers between devices  279 us (38%)
  local copies, waits for them, and re-layouts  154 us (21%)
  matrix products  117 us (16%)
  blocking collectives  95.3 us (13%)
  starting transfers between devices  36 us (5%)
  other arithmetic  28.9 us (4%)
  between operations  14.3 us (2%)
    all_gather x1, waiting for transfers between devices, body(): grads_all = lax.all_gather(key_value_gradients, 'ctx', axis=0, tiled=True)  109 us
    all_gather x1, blocking collectives, body(): places = lax.all_gather(positions, 'ctx', axis=1, tiled=True)[0]  55.8 us
    reduce_scatter x1, waiting for transfers between devices, body(): lax.psum_scatter(row_sum, 'rep', scatter_dimension=1, tiled=True)  42.1 us
    all_to_all x1, blocking collectives, body(): lax.all_to_all(head_query, 'ctx', split_axis=0, concat_axis=1, tiled=True)  39.5 us
    dynamic_update_slice x8, local copies, waits for them, and re-layouts, one_block(): lax.dynamic_update_slice_in_dim(value_acc, lax.dynamic_slice_in_dim(value...  37.7 us
    dynamic_update_slice x8, local copies, waits for them, and re-layouts, one_block(): lax.dynamic_update_slice_in_dim(key_acc, lax.dynamic_slice_in_dim(key_acc...  37.7 us
    unnamed x31, local copies, waits for them, and re-layouts  31.9 us
    all_to_all x1, waiting for transfers between devices, body(): lax.all_to_all(grad_split, 'ctx', split_axis=1, concat_axis=0, tiled=True)  27.9 us
  transfers between devices with their start and end apart: 9, of which 7 were waited for; matrix products, arithmetic and copies ran while one was open for 5% of the time, Pallas kernels for 0%

commit v1 on v0

v1 whole, which is shorter than its diff:
```python
import functools
import math

import jax
import jax.numpy as jnp
from jax import lax
from jax.experimental import pallas as pl
from jax.experimental.pallas import tpu as pltpu
from jax.sharding import PartitionSpec as P

GROUPS = 4
SHARE = 8
D = 128
L = 128
NY, NZL, NZH, NX = 4, 4, 2, 4
HC = 4
ROWS = 256
TILE = 4

F32, BF16 = jnp.float32, jnp.bfloat16
NT = (((1,), (1,)), ((), ()))
TN = (((0,), (0,)), ((), ()))
NN = (((1,), (0,)), ((), ()))


def dot(a, b, dims):
    return lax.dot_general(a, b, dims, preferred_element_type=F32)


def kernel(
    hidden, queries, keys, values, out_grad, positions, dq_out, w_out,
    q_s, go_s, kv, bias, t_s, dp_s, w_s, ds_s, acc, dq_s,
    pair_send, pair_recv, back_send, back_recv, own_s, grads, hid, w_send, w_recv, e_send, e_recv, f_send, f_recv,
    in_sem, dq_sem, a_send, a_recv, af_send, af_recv, h_send, h_recv, h_loc,
    p_ss, p_rs, b_ss, b_rs, g_ss, g_rs, gf_ss, gf_rs, w_ss, w_rs, e_ss, e_rs, f_ss, f_rs,
):
    nctx = NY * NZL * 2
    nz = NZL * NZH
    nb = 2 * HC + 1
    m = NZL * ROWS
    part = D // NY
    tiles = SHARE // TILE
    lanes = TILE * L
    scale = D ** -0.5

    i = lax.axis_index("ctx")
    r = lax.axis_index("rep")
    c = i % 2
    z_lo = (i // 2) % NZL
    y = i // (2 * NZL)
    x = r % NX
    z_hi = r // NX
    zz = z_hi * NZL + z_lo
    sib = i + 1 - 2 * c

    def at(ctx, rep):
        return {"ctx": ctx, "rep": rep}

    def ctx_of(yy, zl, cc):
        return (yy * NZL + zl) * 2 + cc

    def around(d):
        return (i + 2 * d + nctx) % nctx

    def rep_at(d):
        return z_hi * NX + (x + d) % NX

    def y_at(d):
        return (y + d) % NY

    def z_at(d):
        other = (zz + d) % nz
        return other, at(ctx_of(y, other % NZL, c), (other // NZL) * NX + x)

    q_in = pltpu.make_async_copy(queries.at[0], q_s, in_sem.at[0])
    go_in = pltpu.make_async_copy(out_grad.at[0], go_s, in_sem.at[1])
    q_in.start()
    go_in.start()

    barrier = pltpu.get_barrier_semaphore()
    partners = [at(sib, r)]
    for k in range(1, HC + 1):
        partners += [at(around(k), r), at(around(-k), r)]
    for d in range(1, NX):
        partners += [at(i, rep_at(d)), at(sib, rep_at(d))]
    for d in range(1, NY):
        partners.append(at(ctx_of(y_at(d), z_lo, c), r))
    for d in range(1, nz):
        partners.append(z_at(d)[1])
    for partner in partners:
        pl.semaphore_signal(barrier, inc=1, device_id=partner, device_id_type=pl.DeviceIdType.MESH)

    def final_target(g):
        return at(ctx_of(x, z_lo, c), z_hi * NX + g)

    def final_source(q):
        return at(ctx_of(q, z_lo, c), z_hi * NX + y)

    on_diagonal = x == y
    for g in range(NX):
        away = jnp.logical_not(jnp.logical_and(on_diagonal, g == x))

        @pl.when(away)
        def _():
            pl.semaphore_signal(barrier, inc=1, device_id=final_target(g), device_id_type=pl.DeviceIdType.MESH)
            pl.semaphore_signal(barrier, inc=1, device_id=final_source(g), device_id_type=pl.DeviceIdType.MESH)

    for g in range(GROUPS):
        kv[g, HC, c, :, 0:D] = keys[0, :, g * D:(g + 1) * D]
        kv[g, HC, c, :, D:2 * D] = values[0, :, g * D:(g + 1) * D]

    count = len(partners) + 2 * NX - 2 * jnp.where(on_diagonal, 1, 0)
    pl.semaphore_wait(barrier, count)

    def remote(src, dst, send, recv, where):
        return pltpu.make_async_remote_copy(
            src_ref=src, dst_ref=dst, send_sem=send, recv_sem=recv, device_id=where, device_id_type=pl.DeviceIdType.MESH
        )

    def halo(g, k):
        return remote(kv.at[g, HC, c], kv.at[g, HC - k, c], a_send.at[g, k - 1], a_recv.at[g, k - 1], at(around(k), r))

    def pair_kv(g):
        blocks = pl.ds(1 - c, HC)
        return remote(kv.at[g, blocks, c], kv.at[g, blocks, c], af_send.at[g], af_recv.at[g], at(sib, r))

    def pair_kv_in(g):
        blocks = pl.ds(c, HC)
        return remote(kv.at[g, blocks, 1 - c], kv.at[g, blocks, 1 - c], af_send.at[g], af_recv.at[g], at(sib, r))

    for g in range(GROUPS):
        for k in range(1, HC + 1):
            halo(g, k).start()

    def hidden_copy(dx, dc, zl):
        xx = (x + dx) % NX
        cc = (c + dc) % 2
        src = hidden.at[0, :, pl.ds(pl.multiple_of(((xx * NZL + zl) * 2 + cc) * ROWS, ROWS), ROWS)]
        dst = hid.at[2 * x + c, :, pl.ds(zl * ROWS, ROWS)]
        slot = 2 * dx + dc
        if slot == 0:
            return pltpu.make_async_copy(src, dst, h_loc.at[zl])
        return remote(src, dst, h_send.at[slot, zl], h_recv.at[slot, zl], at(ctx_of(y, z_lo, cc), rep_at(dx)))

    for dx in range(NX):
        for dc in range(2):
            for zl in range(NZL):
                hidden_copy(dx, dc, zl).start()

    token = lax.broadcasted_iota(jnp.int32, (L, L), 1) + i * L
    lowest = jnp.maximum(token - jnp.broadcast_to(positions[...], (L, L)), 0)
    for kc in range(nb):
        key = lax.broadcasted_iota(jnp.int32, (L, L), 0) + (i - 2 * HC + kc) * L
        seen = jnp.logical_and(key <= token, key >= lowest)
        bias[kc] = jnp.where(seen, 0.0, -1e30)

    q_in.wait()
    go_in.wait()

    def get_pair_kv(g):
        for k in range(1, HC + 1):
            halo(g, k).wait_recv()
        pair_kv(g).start()

    get_pair_kv(0)

    def attend(t):
        g = t // tiles
        cols = pl.ds(pl.multiple_of(t * lanes, lanes), lanes)
        q_wide = q_s[:, cols]
        go_wide = go_s[:, cols]
        q2 = jnp.concatenate([q_wide[:, j * D:(j + 1) * D] for j in range(TILE)], axis=0)
        go2 = jnp.concatenate([go_wide[:, j * D:(j + 1) * D] for j in range(TILE)], axis=0)

        def block(kc):
            b = c + kc
            return kv[g, b // 2, b % 2]

        def fold(v):
            return v.reshape(L // 8, 8, lanes)

        top = None
        for kc in range(nb):
            s = dot(block(kc)[:, 0:D], q2, NT) + jnp.concatenate([bias[kc]] * TILE, axis=1)
            t_s[kc] = s
            high = jnp.max(fold(s), axis=0)
            top = high if top is None else jnp.maximum(top, high)
        top = jnp.max(top, axis=0, keepdims=True)
        total = jnp.zeros((8, lanes), F32)
        delta = jnp.zeros((8, lanes), F32)
        for kc in range(nb):
            p = jnp.exp2((t_s[kc] - top) * (scale * math.log2(math.e)))
            dp = dot(block(kc)[:, D:2 * D], go2, NT)
            t_s[kc] = p
            dp_s[kc] = dp
            total += jnp.sum(fold(p), axis=0)
            delta += jnp.sum(fold(p * dp), axis=0)
        inverse = 1.0 / jnp.sum(total, axis=0, keepdims=True)
        delta = jnp.sum(delta, axis=0, keepdims=True) * inverse
        for kc in range(nb):
            p = t_s[kc] * inverse
            w_s[kc] = p.astype(BF16)
            ds_s[kc] = (p * (dp_s[kc] - delta)).astype(BF16)
        dq = jnp.zeros((lanes, D), F32)
        for kc in range(nb):
            b = c + kc
            ds = ds_s[kc]
            acc[g % 2, b % 2, b // 2, :, 0:D] += dot(ds, q2, NN)
            acc[g % 2, b % 2, b // 2, :, D:2 * D] += dot(w_s[kc], go2, NN)
            dq += dot(ds, block(kc)[:, 0:D], TN)
        dq = (dq * scale).astype(BF16)
        dq_s[t] = jnp.concatenate([dq[j * L:(j + 1) * L] for j in range(TILE)], axis=1)
        dq_copy(t).start()

    def dq_copy(t):
        cols = pl.ds(pl.multiple_of(t * lanes, lanes), lanes)
        return pltpu.make_async_copy(dq_s.at[t], dq_out.at[0, :, cols], dq_sem.at[t])

    def pair_grads(g):
        return remote(pair_send.at[g, pl.ds(c, HC)], pair_recv.at[g, pl.ds(c, HC)], p_ss.at[g], p_rs.at[g], at(sib, r))

    def pair_grads_in(g):
        blocks = pl.ds(1 - c, HC)
        return remote(pair_send.at[g, blocks], pair_recv.at[g, blocks], p_ss.at[g], p_rs.at[g], at(sib, r))

    def stage0(g):
        pair_send[g] = acc[g % 2, 1 - c].astype(BF16)
        pair_recv[g, HC * c] = jnp.zeros((L, 2 * D), BF16)
        pair_grads(g).start()

    def back(g, k):
        return remote(back_send.at[g, k], back_recv.at[g, k], b_ss.at[g, k], b_rs.at[g, k], at(around(k - HC), r))

    def stage1(g):
        pair_grads_in(g).wait_recv()
        for k in range(HC):
            back_send[g, k] = (acc[g % 2, c, k] + pair_recv[g, k].astype(F32)).astype(BF16)
            back(g, k).start()
        own_s[...] = acc[g % 2, c, HC] + pair_recv[g, HC].astype(F32)

    def spread(g, d):
        mine = grads.at[g, x, c]
        return remote(mine, mine, g_ss.at[g, d - 1], g_rs.at[g, d - 1], at(i, rep_at(d)))

    def stage2(g):
        whole = own_s[...]
        for k in range(HC):
            back(g, k).wait_recv()
            whole += back_recv[g, k].astype(F32)
        grads[g, x, c, :, 0:D] = (whole[:, 0:D] * scale).astype(BF16)
        grads[g, x, c, :, D:2 * D] = whole[:, D:2 * D].astype(BF16)
        for d in range(1, NX):
            spread(g, d).start()

    def pair_spread(g, cc):
        half = grads.at[g, :, cc]
        return remote(half, half, gf_ss.at[g], gf_rs.at[g], at(sib, r))

    def stage3(g):
        for d in range(1, NX):
            spread(g, d).wait_recv()
        pair_spread(g, c).start()

    def w_copy(g, d):
        return remote(w_send.at[g, y_at(d)], w_recv.at[g, d - 1], w_ss.at[g, d - 1], w_rs.at[g, d - 1],
                      at(ctx_of(y_at(d), z_lo, c), r))

    def stage4(g):
        @pl.when(g == 0)
        def _():
            for dx in range(NX):
                for dc in range(2):
                    for zl in range(NZL):
                        copy = hidden_copy(dx, dc, zl)
                        copy.wait() if dx + dc == 0 else copy.wait_recv()

        pair_spread(g, 1 - c).wait_recv()
        tokens = NX * 2 * L
        got = dot(grads[g].reshape(tokens, 2 * D), hid[...].reshape(tokens, m), TN).astype(BF16)
        for j in range(NY):
            w_send[g, j, 0:part] = got[j * part:(j + 1) * part]
            w_send[g, j, part:2 * part] = got[D + j * part:D + (j + 1) * part]
        for d in range(1, NY):
            w_copy(g, d).start()

    def e_copy(g, d):
        other, where = z_at(d)
        return remote(e_send.at[g, other], e_recv.at[g, d - 1], e_ss.at[g, d - 1], e_rs.at[g, d - 1], where)

    def stage5(g):
        whole = w_send[g, y].astype(F32)
        for d in range(1, NY):
            w_copy(g, d).wait_recv()
            whole += w_recv[g, d - 1].astype(F32)
        for zh in range(NZH):
            for zl in range(NZL):
                e_send[g, zh * NZL + zl] = whole[zh * part:(zh + 1) * part, zl * ROWS:(zl + 1) * ROWS].astype(BF16)
        for d in range(1, nz):
            e_copy(g, d).start()

    def f_copy(g):
        return remote(f_send.at[g], f_recv.at[y], f_ss.at[g], f_rs.at[y], final_target(g))

    def stays(g):
        return jnp.logical_and(on_diagonal, g == x)

    def stage6(g):
        whole = e_send[g, zz].astype(F32)
        for d in range(1, nz):
            e_copy(g, d).wait_recv()
            whole += e_recv[g, d - 1].astype(F32)

        @pl.when(stays(g))
        def _():
            f_recv[y] = whole

        @pl.when(jnp.logical_not(stays(g)))
        def _():
            f_send[g] = whole
            f_copy(g).start()

    stages = (stage0, stage1, stage2, stage3, stage4, stage5, stage6)

    def step(t, nothing):
        @pl.when(t < GROUPS * tiles)
        def _():
            g = t // tiles

            @pl.when(t % tiles == 0)
            def _():
                acc[g % 2] = jnp.zeros((2, HC + 1, L, 2 * D), F32)
                pair_kv_in(g).wait_recv()

                @pl.when(g + 1 < GROUPS)
                def _():
                    get_pair_kv(g + 1)

            attend(t)

        for s, stage in enumerate(stages):
            since = t - s - (tiles - 1)

            @pl.when(jnp.logical_and(since % tiles == 0, jnp.logical_and(since >= 0, since < GROUPS * tiles)))
            def _():
                stage(since // tiles)

        return nothing

    lax.fori_loop(0, (GROUPS - 1) * tiles + tiles - 1 + len(stages), step, 0)

    for q in range(NY):
        here = jnp.logical_and(on_diagonal, q == y)

        @pl.when(jnp.logical_not(here))
        def _():
            remote(f_send.at[0], f_recv.at[q], f_ss.at[0], f_rs.at[q], final_source(q)).wait_recv()

    w_out[...] = jnp.transpose(f_recv[...].reshape(D, ROWS))

    for t in range(GROUPS * tiles):
        dq_copy(t).wait()
    for g in range(GROUPS):
        for k in range(1, HC + 1):
            halo(g, k).wait_send()
        pair_kv(g).wait_send()
        pair_grads(g).wait_send()
        for k in range(HC):
            back(g, k).wait_send()
        for d in range(1, NX):
            spread(g, d).wait_send()
        pair_spread(g, c).wait_send()
        for d in range(1, NY):
            w_copy(g, d).wait_send()
        for d in range(1, nz):
            e_copy(g, d).wait_send()

        @pl.when(jnp.logical_not(stays(g)))
        def _():
            f_copy(g).wait_send()

    for dx in range(NX):
        for dc in range(2):
            for zl in range(NZL):
                if dx + dc:
                    hidden_copy(dx, dc, zl).wait_send()


def body(hidden, queries, keys, values, out_grad, positions):
    nb, nz, m, part = 2 * HC + 1, NZL * NZH, NZL * ROWS, D // NY
    tiles, lanes = SHARE // TILE, TILE * L
    vmem, dma = pltpu.VMEM, pltpu.SemaphoreType.DMA
    anywhere, inside = pl.BlockSpec(memory_space=pl.ANY), pl.BlockSpec(memory_space=pltpu.VMEM)
    pairs = GROUPS * SHARE * L * L * nb
    return pl.pallas_call(
        kernel,
        out_shape=(
            jax.ShapeDtypeStruct(queries.shape, BF16),
            jax.ShapeDtypeStruct((ROWS, D), F32),
        ),
        in_specs=[anywhere, anywhere, inside, inside, anywhere, inside],
        out_specs=(anywhere, inside),
        scratch_shapes=[
            vmem(queries.shape[1:], BF16),
            vmem(queries.shape[1:], BF16),
            vmem((GROUPS, HC + 1, 2, L, 2 * D), BF16),
            vmem((nb, L, L), F32),
            vmem((nb, L, lanes), F32),
            vmem((nb, L, lanes), F32),
            vmem((nb, L, lanes), BF16),
            vmem((nb, L, lanes), BF16),
            vmem((2, 2, HC + 1, L, 2 * D), F32),
            vmem((GROUPS * tiles, L, lanes), BF16),
            vmem((GROUPS, HC + 1, L, 2 * D), BF16),
            vmem((GROUPS, HC + 1, L, 2 * D), BF16),
            vmem((GROUPS, HC, L, 2 * D), BF16),
            vmem((GROUPS, HC, L, 2 * D), BF16),
            vmem((L, 2 * D), F32),
            vmem((GROUPS, NX, 2, L, 2 * D), BF16),
            vmem((NX * 2, L, m), BF16),
            vmem((GROUPS, NY, 2 * part, m), BF16),
            vmem((GROUPS, NY - 1, 2 * part, m), BF16),
            vmem((GROUPS, nz, part, ROWS), BF16),
            vmem((GROUPS, nz - 1, part, ROWS), BF16),
            vmem((GROUPS, part, ROWS), F32),
            vmem((NY, part, ROWS), F32),
            dma((2,)),
            dma((GROUPS * tiles,)),
            dma((GROUPS, HC)), dma((GROUPS, HC)),
            dma((GROUPS,)), dma((GROUPS,)),
            dma((2 * NX, NZL)), dma((2 * NX, NZL)), dma((NZL,)),
            dma((GROUPS,)), dma((GROUPS,)),
            dma((GROUPS, HC)), dma((GROUPS, HC)),
            dma((GROUPS, NX - 1)), dma((GROUPS, NX - 1)),
            dma((GROUPS,)), dma((GROUPS,)),
            dma((GROUPS, NY - 1)), dma((GROUPS, NY - 1)),
            dma((GROUPS, nz - 1)), dma((GROUPS, nz - 1)),
            dma((GROUPS,)), dma((NY,)),
        ],
        compiler_params=pltpu.CompilerParams(
            collective_id=0, has_side_effects=True, vmem_limit_bytes=56 * 2**20
        ),
        cost_estimate=pl.CostEstimate(
            flops=10 * pairs * D, bytes_accessed=12 * 2**20, transcendentals=pairs
        ),
    )(hidden, queries, keys, values, out_grad, positions)


def solution(mesh):
    rows = P("rep", "ctx", None)
    return jax.shard_map(
        body,
        mesh=mesh,
        in_specs=(rows, rows, rows, rows, rows, P("rep", "ctx")),
        out_specs=(rows, P("ctx", "rep")),
        check_vma=False,
    )
```

time: 736 us -> 114 us (0.15)
  waiting for transfers between devices: 279 us -> 0 us
  local copies, waits for them, and re-layouts: 154 us -> 2.98 us
  matrix products: 117 us -> 0 us
  Pallas kernels: 0 us -> 110 us
  blocking collectives: 95.3 us -> 0 us
  starting transfers between devices: 36 us -> 0 us
  other arithmetic: 28.9 us -> 0 us
  between operations: 14.3 us -> 0.65 us
    all_to_all x7 -> x0, waiting for transfers between devices: 128 us -> none  [the longest x1 27.9 us: body(): lax.all_to_all(grad_split, 'ctx', split_axis=1, concat_axis=0, tiled=True)]
    dot_general x56 -> x0, matrix products: 117 us -> none  [the longest x8 20.4 us: one_block(): jnp.einsum('hqk,qhd->khd', dscore, query_block, preferred_element_type=jn...]
    pallas_call x0 -> x1, Pallas kernels: none -> 110 us  [body(): pl.pallas_call(kernel, out_shape=(jax.ShapeDtypeStruct(queries.shape, BF1...]
    all_gather x1 -> x0, waiting for transfers between devices: 109 us -> none  [body(): grads_all = lax.all_gather(key_value_gradients, 'ctx', axis=0, tiled=True)]
    dynamic_update_slice x32 -> x0, local copies, waits for them, and re-layouts: 81.7 us -> none  [the longest x8 37.7 us: one_block(): lax.dynamic_update_slice_in_dim(value_acc, lax.dynamic_slice_in_dim(value...]
    all_gather x1 -> x0, blocking collectives: 55.8 us -> none  [body(): places = lax.all_gather(positions, 'ctx', axis=1, tiled=True)[0]]
    reduce_scatter x1 -> x0, waiting for transfers between devices: 42.1 us -> none  [body(): lax.psum_scatter(row_sum, 'rep', scatter_dimension=1, tiled=True)]
    all_to_all x1 -> x0, blocking collectives: 39.5 us -> none  [body(): lax.all_to_all(head_query, 'ctx', split_axis=0, concat_axis=1, tiled=True)]
  transfers between devices with their start and end apart: 9 -> 0, of which waited for: 7 -> 0; matrix products, arithmetic and copies ran while one was open for 5% -> 0% of each run, Pallas kernels for 0% -> 0%
where the time goes in v1:
time: 114 us; the launch traced here: 113 us
  Pallas kernels  110 us (96%)
  local copies, waits for them, and re-layouts  2.98 us (3%)
    pallas_call x1, Pallas kernels, body(): pl.pallas_call(kernel, out_shape=(jax.ShapeDtypeStruct(queries.shape, BF1...  110 us
    unnamed x4, local copies, waits for them, and re-layouts  2.98 us

profile of v1, /device:TPU:6, one launch (start us, length us, event | category | flops | bytes accessed | tf_op | source)
XLA Modules:
  0.0 113.5 jit_solution(13828217138373659665)
XLA Ops:
  0.6 109.9 %shard_map.77 = (bf16[1,128,4096]{2,1,0:T(8,128)(2,1)}, f32[256,128]{1,0:T(8,128)}) custom-call(bf16[1,128,8192]{2,1,0:T(8,128)(2,1)} %hidden.1, bf16[1,128,4096]{2,1,0:T(8,128)(2,1)} %queries.1, bf16[1,128,512]{2,1,0:T(8,128)(2,1)} %keys.1, bf16[1,128,512]{2,1,0:T(8,128)(2,1)} %values.1, bf16[1,128,4096]{2,1,0:T(8,128)(2,1)} %out_grad.1, s32[1,128]{1,0:T(1,128)} %positions.1), custom_call_target="tpu_custom_call" | custom-call | flops 6039797760 | bytes 12582912 | tf_op jit(solution)/shard_map/pallas_call | solution.py:394
  110.5 0.0 copy-start
  110.5 2.3 %copy.10 = bf16[1,128,4096]{2,1,0:T(8,128)(2,1)} copy(bf16[1,128,4096]{2,1,0:T(8,128)(2,1)} %get-tuple-element.4) | data formatting | bytes 2097152
  112.8 0.0 copy-done
  112.8 0.7 copy.11
Async XLA Ops:
  110.5 2.3 %copy-start = (f32[256,128]{1,0:T(8,128)S(1)}, f32[256,128]{1,0:T(8,128)}, u32[]{:S(2)}) copy-start(f32[256,128]{1,0:T(8,128)} %get-tuple-element.5) | copy-start | bytes 393220

commit v2 on v1

--- a/solution.py
+++ b/solution.py
@@ -16,6 +16,7 @@
 HC = 4
 ROWS = 256
 TILE = 4
+WHEN = ((1, 2), (2, 2), (4, 2), (7, 1), (8, 1), (8, 1), (10, 1), (11, 1))
 
 F32, BF16 = jnp.float32, jnp.bfloat16
 NT = (((1,), (1,)), ((), ()))
@@ -30,9 +31,9 @@
 def kernel(
     hidden, queries, keys, values, out_grad, positions, dq_out, w_out,
     q_s, go_s, kv, bias, t_s, dp_s, w_s, ds_s, acc, dq_s,
-    pair_send, pair_recv, back_send, back_recv, own_s, grads, hid, w_send, w_recv, e_send, e_recv, f_send, f_recv,
-    in_sem, dq_sem, a_send, a_recv, af_send, af_recv, h_send, h_recv, h_loc,
-    p_ss, p_rs, b_ss, b_rs, g_ss, g_rs, gf_ss, gf_rs, w_ss, w_rs, e_ss, e_rs, f_ss, f_rs,
+    pair_send, pair_recv, back_send, back_recv, relay_recv, own_s, grads, hid, w_send, w_recv, e_send, e_recv, f_send, f_recv,
+    in_sem, dq_sem, a_send, a_recv, fw_send, af_send, af_recv, h_send, h_recv, h_loc,
+    p_ss, p_rs, r_ss, r_rs, b_ss, b_rs, g_ss, g_rs, gf_ss, gf_rs, w_ss, w_rs, e_ss, e_rs, f_ss, f_rs,
 ):
     nctx = NY * NZL * 2
     nz = NZL * NZH
@@ -128,9 +129,40 @@
         blocks = pl.ds(c, HC)
         return remote(kv.at[g, blocks, 1 - c], kv.at[g, blocks, 1 - c], af_send.at[g], af_recv.at[g], at(sib, r))
 
-    for g in range(GROUPS):
+    def direct(k):
+        there = z_lo + k
+        along = jnp.logical_and(there < NZL, jnp.logical_or(there < NZL - 1, k == 1))
+        down = jnp.logical_and(there >= NZL, jnp.logical_or((there - NZL) % NZL > 0, k == HC))
+        return jnp.logical_or(along, down)
+
+    def to_last(g, k):
+        there = at(around(1), r)
+        return remote(kv.at[g, HC - k, c], kv.at[g, HC - k - 1, c], fw_send.at[g, k - 1], a_recv.at[g, k], there)
+
+    def to_first(g, k):
+        there = at(around(-1), r)
+        return remote(kv.at[g, HC - k, c], kv.at[g, HC - k + 1, c], fw_send.at[g, k - 1], a_recv.at[g, k - 2], there)
+
+    passes_last = jnp.logical_and(z_lo == NZL - 2, NZL > 2)
+    passes_first = z_lo == 1
+    last_by = range(1, NZL - 1)
+    first_by = range(2, HC + 1)
+
+    def send_kv(g):
         for k in range(1, HC + 1):
-            halo(g, k).start()
+
+            @pl.when(jnp.logical_or(g == 0, direct(k)))
+            def _():
+                halo(g, k).start()
+
+    def kv_sent(g):
+        for k in range(1, HC + 1):
+
+            @pl.when(jnp.logical_or(g == 0, direct(k)))
+            def _():
+                halo(g, k).wait_send()
+
+    send_kv(0)
 
     def hidden_copy(dx, dc, zl):
         xx = (x + dx) % NX
@@ -157,12 +189,37 @@
     q_in.wait()
     go_in.wait()
 
-    def get_pair_kv(g):
+
+    def passes(k):
+        return jnp.logical_or(
+            jnp.logical_and(passes_last, k in last_by), jnp.logical_and(passes_first, k in first_by)
+        )
+
+    def pass_on(g):
+        @pl.when(passes_last)
+        def _():
+            for k in last_by:
+                halo(g, k).wait_recv()
+                to_last(g, k).start()
+
+        @pl.when(passes_first)
+        def _():
+            for k in reversed(first_by):
+                halo(g, k).wait_recv()
+                to_first(g, k).start()
+
+    def to_pair(g):
         for k in range(1, HC + 1):
-            halo(g, k).wait_recv()
+
+            @pl.when(jnp.logical_or(g == 0, jnp.logical_not(passes(k))))
+            def _():
+                halo(g, k).wait_recv()
+
         pair_kv(g).start()
 
-    get_pair_kv(0)
+    kv_sent(0)
+    send_kv(1)
+    to_pair(0)
 
     def attend(t):
         g = t // tiles
@@ -231,22 +288,80 @@
     def back(g, k):
         return remote(back_send.at[g, k], back_recv.at[g, k], b_ss.at[g, k], b_rs.at[g, k], at(around(k - HC), r))
 
+    def comes_direct(k):
+        along = jnp.logical_and(k <= z_lo, jnp.logical_or(z_lo < NZL - 1, k == 1))
+        down = jnp.logical_and(k > z_lo, jnp.logical_or(z_lo > 0, k == HC))
+        return jnp.logical_or(along, down)
+
+    def relayed(g):
+        return g < GROUPS - 1
+
+    def relay_down(g, k):
+        return remote(back_send.at[g, HC - k], relay_recv.at[g, k - 2], r_ss.at[g, k - 1], r_rs.at[g, k - 2], at(around(-1), r))
+
+    def relay_up(g, k):
+        return remote(back_send.at[g, HC - k], relay_recv.at[g, k - 1], r_ss.at[g, k - 1], r_rs.at[g, k - 1], at(around(1), r))
+
+    def relay_roles(g, k):
+        by = jnp.logical_and(relayed(g), jnp.logical_not(comes_direct(k)))
+        holds = jnp.logical_and(relayed(g), passes(k))
+        return by, holds, jnp.logical_not(jnp.logical_or(by, holds))
+
     def stage1(g):
         pair_grads_in(g).wait_recv()
-        for k in range(HC):
-            back_send[g, k] = (acc[g % 2, c, k] + pair_recv[g, k].astype(F32)).astype(BF16)
-            back(g, k).start()
-        own_s[...] = acc[g % 2, c, HC] + pair_recv[g, HC].astype(F32)
+        for k in range(1, HC + 1):
+            n = HC - k
+            back_send[g, n] = (acc[g % 2, c, n] + pair_recv[g, n].astype(F32)).astype(BF16)
+            by, holds, plain = relay_roles(g, k)
+
+            @pl.when(plain)
+            def _():
+                back(g, n).start()
+
+            if k >= 2:
+
+                @pl.when(jnp.logical_and(by, z_lo == NZL - 1))
+                def _():
+                    relay_down(g, k).start()
+
+            if k < HC:
+
+                @pl.when(jnp.logical_and(by, z_lo == 0))
+                def _():
+                    relay_up(g, k).start()
+
+        own_s[g] = acc[g % 2, c, HC] + pair_recv[g, HC].astype(F32)
+
+    def stage1b(g):
+        def add_and_send(k, copy, slot):
+            copy.wait_recv()
+            n = HC - k
+            back_send[g, n] = (back_send[g, n].astype(F32) + relay_recv[g, slot].astype(F32)).astype(BF16)
+            back(g, n).start()
+
+        @pl.when(jnp.logical_and(relayed(g), passes_last))
+        def _():
+            for k in last_by:
+                add_and_send(k, relay_down(g, k + 1), k - 1)
+
+        @pl.when(jnp.logical_and(relayed(g), passes_first))
+        def _():
+            for k in first_by:
+                add_and_send(k, relay_up(g, k - 1), k - 2)
 
     def spread(g, d):
         mine = grads.at[g, x, c]
         return remote(mine, mine, g_ss.at[g, d - 1], g_rs.at[g, d - 1], at(i, rep_at(d)))
 
     def stage2(g):
-        whole = own_s[...]
-        for k in range(HC):
-            back(g, k).wait_recv()
-            whole += back_recv[g, k].astype(F32)
+        for k in range(1, HC + 1):
+
+            @pl.when(jnp.logical_or(jnp.logical_not(relayed(g)), direct(k)))
+            def _():
+                back(g, HC - k).wait_recv()
+                own_s[g] += back_recv[g, HC - k].astype(F32)
+
+        whole = own_s[g]
         grads[g, x, c, :, 0:D] = (whole[:, 0:D] * scale).astype(BF16)
         grads[g, x, c, :, D:2 * D] = whole[:, D:2 * D].astype(BF16)
         for d in range(1, NX):
@@ -319,10 +434,12 @@
             f_send[g] = whole
             f_copy(g).start()
 
-    stages = (stage0, stage1, stage2, stage3, stage4, stage5, stage6)
+    stages = (stage0, stage1, stage1b, stage2, stage3, stage4, stage5, stage6)
+
+    slots = GROUPS * tiles
 
     def step(t, nothing):
-        @pl.when(t < GROUPS * tiles)
+        @pl.when(t < slots)
         def _():
             g = t // tiles
 
@@ -331,22 +448,30 @@
                 acc[g % 2] = jnp.zeros((2, HC + 1, L, 2 * D), F32)
                 pair_kv_in(g).wait_recv()
 
-                @pl.when(g + 1 < GROUPS)
-                def _():
-                    get_pair_kv(g + 1)
-
             attend(t)
 
-        for s, stage in enumerate(stages):
-            since = t - s - (tiles - 1)
-
-            @pl.when(jnp.logical_and(since % tiles == 0, jnp.logical_and(since >= 0, since < GROUPS * tiles)))
-            def _():
-                stage(since // tiles)
+            @pl.when(jnp.logical_and(t % tiles == tiles - 1, g + 1 < GROUPS))
+            def _():
+                to_pair(g + 1)
+
+            @pl.when(t + 2 < GROUPS)
+            def _():
+                send_kv(t + 2)
+
+            @pl.when(t + 1 < GROUPS)
+            def _():
+                pass_on(t + 1)
+
+        for (first, pace), stage in zip(WHEN, stages):
+            since = t - first
+
+            @pl.when(jnp.logical_and(since % pace == 0, jnp.logical_and(since >= 0, since < GROUPS * pace)))
+            def _():
+                stage(since // pace)
 
         return nothing
 
-    lax.fori_loop(0, (GROUPS - 1) * tiles + tiles - 1 + len(stages), step, 0)
+    lax.fori_loop(0, WHEN[-1][0] + (GROUPS - 1) * WHEN[-1][1] + 1, step, 0)
 
     for q in range(NY):
         here = jnp.logical_and(on_diagonal, q == y)
@@ -360,12 +485,40 @@
     for t in range(GROUPS * tiles):
         dq_copy(t).wait()
     for g in range(GROUPS):
-        for k in range(1, HC + 1):
-            halo(g, k).wait_send()
+        if g > 0:
+            kv_sent(g)
+
+            @pl.when(passes_last)
+            def _():
+                for k in last_by:
+                    to_last(g, k).wait_send()
+
+            @pl.when(passes_first)
+            def _():
+                for k in first_by:
+                    to_first(g, k).wait_send()
+
         pair_kv(g).wait_send()
         pair_grads(g).wait_send()
-        for k in range(HC):
-            back(g, k).wait_send()
+        for k in range(1, HC + 1):
+            by, holds, plain = relay_roles(g, k)
+
+            @pl.when(jnp.logical_not(by))
+            def _():
+                back(g, HC - k).wait_send()
+
+            if k >= 2 and g < GROUPS - 1:
+
+                @pl.when(jnp.logical_and(by, z_lo == NZL - 1))
+                def _():
+                    relay_down(g, k).wait_send()
+
+            if k < HC and g < GROUPS - 1:
+
+                @pl.when(jnp.logical_and(by, z_lo == 0))
+                def _():
+                    relay_up(g, k).wait_send()
+
         for d in range(1, NX):
             spread(g, d).wait_send()
         pair_spread(g, c).wait_send()
@@ -414,7 +567,8 @@
             vmem((GROUPS, HC + 1, L, 2 * D), BF16),
             vmem((GROUPS, HC, L, 2 * D), BF16),
             vmem((GROUPS, HC, L, 2 * D), BF16),
-            vmem((L, 2 * D), F32),
+            vmem((GROUPS, HC - 1, L, 2 * D), BF16),
+            vmem((GROUPS, L, 2 * D), F32),
             vmem((GROUPS, NX, 2, L, 2 * D), BF16),
             vmem((NX * 2, L, m), BF16),
             vmem((GROUPS, NY, 2 * part, m), BF16),
@@ -425,10 +579,11 @@
             vmem((NY, part, ROWS), F32),
             dma((2,)),
             dma((GROUPS * tiles,)),
-            dma((GROUPS, HC)), dma((GROUPS, HC)),
+            dma((GROUPS, HC)), dma((GROUPS, HC)), dma((GROUPS, HC)),
             dma((GROUPS,)), dma((GROUPS,)),
             dma((2 * NX, NZL)), dma((2 * NX, NZL)), dma((NZL,)),
             dma((GROUPS,)), dma((GROUPS,)),
+            dma((GROUPS, HC)), dma((GROUPS, HC - 1)),
             dma((GROUPS, HC)), dma((GROUPS, HC)),
             dma((GROUPS, NX - 1)), dma((GROUPS, NX - 1)),
             dma((GROUPS,)), dma((GROUPS,)),

time: 114 us -> 102 us (0.89)
  Pallas kernels: 110 us -> 98 us
    pallas_call x1, Pallas kernels: 110 us -> 98 us  [body(): pl.pallas_call(kernel, out_shape=(jax.ShapeDtypeStruct(queries.shape, BF1...]
where the time goes in v2:
time: 102 us
  Pallas kernels  98 us (96%)
  local copies, waits for them, and re-layouts  2.98 us (3%)
    pallas_call x1, Pallas kernels, body(): pl.pallas_call(kernel, out_shape=(jax.ShapeDtypeStruct(queries.shape, BF1...  98 us
    unnamed x4, local copies, waits for them, and re-layouts  2.98 us

profile of v2, /device:TPU:6, one launch (start us, length us, event | category | flops | bytes accessed | tf_op | source)
XLA Modules:
  0.0 101.6 jit_solution(5733660208405018334)
XLA Ops:
  0.6 98.0 %shard_map.77 = (bf16[1,128,4096]{2,1,0:T(8,128)(2,1)}, f32[256,128]{1,0:T(8,128)}) custom-call(bf16[1,128,8192]{2,1,0:T(8,128)(2,1)} %hidden.1, bf16[1,128,4096]{2,1,0:T(8,128)(2,1)} %queries.1, bf16[1,128,512]{2,1,0:T(8,128)(2,1)} %keys.1, bf16[1,128,512]{2,1,0:T(8,128)(2,1)} %values.1, bf16[1,128,4096]{2,1,0:T(8,128)(2,1)} %out_grad.1, s32[1,128]{1,0:T(1,128)} %positions.1), custom_call_target="tpu_custom_call" | custom-call | flops 6039797760 | bytes 12582912 | tf_op jit(solution)/shard_map/pallas_call | solution.py:547
  98.6 0.0 copy-start
  98.6 2.3 %copy.10 = bf16[1,128,4096]{2,1,0:T(8,128)(2,1)} copy(bf16[1,128,4096]{2,1,0:T(8,128)(2,1)} %get-tuple-element.4) | data formatting | bytes 2097152
  101.0 0.0 copy-done
  101.0 0.7 copy.11
Async XLA Ops:
  98.6 2.3 %copy-start = (f32[256,128]{1,0:T(8,128)S(1)}, f32[256,128]{1,0:T(8,128)}, u32[]{:S(2)}) copy-start(f32[256,128]{1,0:T(8,128)} %get-tuple-element.5) | copy-start | bytes 393220

commit v3 on v2

--- a/solution.py
+++ b/solution.py
@@ -15,8 +15,11 @@
 NY, NZL, NZH, NX = 4, 4, 2, 4
 HC = 4
 ROWS = 256
+COPIES = 4
 TILE = 4
-WHEN = ((1, 2), (2, 2), (4, 2), (7, 1), (8, 1), (8, 1), (10, 1), (11, 1))
+WHEN = (
+    (1, 3, 5, 7), (2, 4, 6, 8), (4, 6, 8, 8), (7, 8, 9, 10), (8, 9, 10, 11), (8, 9, 10, 11), (11, 11, 11, 12), (12, 12, 12, 13),
+)
 
 F32, BF16 = jnp.float32, jnp.bfloat16
 NT = (((1,), (1,)), ((), ()))
@@ -462,16 +465,19 @@
             def _():
                 pass_on(t + 1)
 
-        for (first, pace), stage in zip(WHEN, stages):
-            since = t - first
-
-            @pl.when(jnp.logical_and(since % pace == 0, jnp.logical_and(since >= 0, since < GROUPS * pace)))
-            def _():
-                stage(since // pace)
+        for when, stage in zip(WHEN, stages):
+            begun = sum((t > slot).astype(jnp.int32) for slot in when[:GROUPS])
+            due = sum((t >= slot).astype(jnp.int32) for slot in when[:GROUPS])
+
+            def one(g, nothing, stage=stage):
+                stage(g)
+                return nothing
+
+            lax.fori_loop(begun, due, one, 0)
 
         return nothing
 
-    lax.fori_loop(0, WHEN[-1][0] + (GROUPS - 1) * WHEN[-1][1] + 1, step, 0)
+    lax.fori_loop(0, WHEN[-1][-1] + 1, step, 0)
 
     for q in range(NY):
         here = jnp.logical_and(on_diagonal, q == y)
@@ -538,13 +544,30 @@
                     hidden_copy(dx, dc, zl).wait_send()
 
 
+def hand_over(dq, w, dq_out, w_out, dq_s, w_s, sem_in, sem_out):
+    rows = L // COPIES
+    parts = [(w, w_s, w_out)]
+    for n in range(COPIES):
+        part = pl.ds(n * rows, rows)
+        parts.append((dq.at[0, part], dq_s.at[part], dq_out.at[0, part]))
+    ins = [pltpu.make_async_copy(a, b, sem_in.at[n]) for n, (a, b, _) in enumerate(parts)]
+    outs = [pltpu.make_async_copy(b, o, sem_out.at[n]) for n, (_, b, o) in enumerate(parts)]
+    for copy in ins:
+        copy.start()
+    for arrived, copy in zip(ins, outs):
+        arrived.wait()
+        copy.start()
+    for copy in outs:
+        copy.wait()
+
+
 def body(hidden, queries, keys, values, out_grad, positions):
     nb, nz, m, part = 2 * HC + 1, NZL * NZH, NZL * ROWS, D // NY
     tiles, lanes = SHARE // TILE, TILE * L
     vmem, dma = pltpu.VMEM, pltpu.SemaphoreType.DMA
     anywhere, inside = pl.BlockSpec(memory_space=pl.ANY), pl.BlockSpec(memory_space=pltpu.VMEM)
     pairs = GROUPS * SHARE * L * L * nb
-    return pl.pallas_call(
+    results = pl.pallas_call(
         kernel,
         out_shape=(
             jax.ShapeDtypeStruct(queries.shape, BF16),
@@ -598,6 +621,13 @@
             flops=10 * pairs * D, bytes_accessed=12 * 2**20, transcendentals=pairs
         ),
     )(hidden, queries, keys, values, out_grad, positions)
+    return pl.pallas_call(
+        hand_over,
+        out_shape=tuple(jax.ShapeDtypeStruct(a.shape, a.dtype) for a in results),
+        in_specs=[anywhere, anywhere],
+        out_specs=(anywhere, anywhere),
+        scratch_shapes=[vmem(queries.shape[1:], BF16), vmem((ROWS, D), F32), dma((COPIES + 1,)), dma((COPIES + 1,))],
+    )(*results)
 
 
 def solution(mesh):

time: 102 us -> 99.8 us (0.978)
  local copies, waits for them, and re-layouts: 2.98 us -> 0 us
    unnamed x4 -> x0, local copies, waits for them, and re-layouts: 2.98 us -> none
    pallas_call x0 -> x1, Pallas kernels: none -> 2.07 us  [body(): pl.pallas_call(hand_over, out_shape=tuple((jax.ShapeDtypeStruct(a.shape,...]
    pallas_call x1, Pallas kernels: 98 us -> 96.9 us  [body(): pl.pallas_call(kernel, out_shape=(jax.ShapeDtypeStruct(queries.shape, BF1...]
where the time goes in v3:
time: 99.8 us; the launch traced here: 99.6 us
  Pallas kernels  99 us (99%)
    pallas_call x1, Pallas kernels, body(): pl.pallas_call(kernel, out_shape=(jax.ShapeDtypeStruct(queries.shape, BF1...  96.9 us
    pallas_call x1, Pallas kernels, body(): pl.pallas_call(hand_over, out_shape=tuple((jax.ShapeDtypeStruct(a.shape,...  2.07 us

profile of v3, /device:TPU:6, one launch (start us, length us, event | category | flops | bytes accessed | tf_op | source)
XLA Modules:
  0.0 99.6 jit_solution(251278596770033386)
XLA Ops:
  0.6 96.9 %shard_map.77 = (bf16[1,128,4096]{2,1,0:T(8,128)(2,1)}, f32[256,128]{1,0:T(8,128)}) custom-call(bf16[1,128,8192]{2,1,0:T(8,128)(2,1)} %hidden.1, bf16[1,128,4096]{2,1,0:T(8,128)(2,1)} %queries.1, bf16[1,128,512]{2,1,0:T(8,128)(2,1)} %keys.1, bf16[1,128,512]{2,1,0:T(8,128)(2,1)} %values.1, bf16[1,128,4096]{2,1,0:T(8,128)(2,1)} %out_grad.1, s32[1,128]{1,0:T(1,128)} %positions.1), custom_call_target="tpu_custom_call" | custom-call | flops 6039797760 | bytes 12582912 | tf_op jit(solution)/shard_map/pallas_call | solution.py:570
  97.6 2.1 %shard_map.78 = (bf16[1,128,4096]{2,1,0:T(8,128)(2,1)}, f32[256,128]{1,0:T(8,128)}) custom-call(bf16[1,128,4096]{2,1,0:T(8,128)(2,1)} %get-tuple-element.4.dq, f32[256,128]{1,0:T(8,128)} %get-tuple-element.5.w), custom_call_target="tpu_custom_call" | custom-call | tf_op jit(solution)/shard_map/pallas_call | solution.py:624

commit v4 on v3

--- a/solution.py
+++ b/solution.py
@@ -18,7 +18,7 @@
 COPIES = 4
 TILE = 4
 WHEN = (
-    (1, 3, 5, 7), (2, 4, 6, 8), (4, 6, 8, 8), (7, 8, 9, 10), (8, 9, 10, 11), (8, 9, 10, 11), (11, 11, 11, 12), (12, 12, 12, 13),
+    (1, 3, 5, 7), (2, 4, 6, 8), (4, 6, 8, 8), (7, 8, 9, 10), (8, 9, 10, 11), (8, 9, 10, 11), (11, 11, 12, 12), (12, 12, 13, 13),
 )
 
 F32, BF16 = jnp.float32, jnp.bfloat16
@@ -297,7 +297,7 @@
         return jnp.logical_or(along, down)
 
     def relayed(g):
-        return g < GROUPS - 1
+        return jnp.logical_and(g >= 1, g < GROUPS - 1)
 
     def relay_down(g, k):
         return remote(back_send.at[g, HC - k], relay_recv.at[g, k - 2], r_ss.at[g, k - 1], r_rs.at[g, k - 2], at(around(-1), r))
@@ -513,13 +513,13 @@
             def _():
                 back(g, HC - k).wait_send()
 
-            if k >= 2 and g < GROUPS - 1:
+            if k >= 2 and 1 <= g < GROUPS - 1:
 
                 @pl.when(jnp.logical_and(by, z_lo == NZL - 1))
                 def _():
                     relay_down(g, k).wait_send()
 
-            if k < HC and g < GROUPS - 1:
+            if k < HC and 1 <= g < GROUPS - 1:
 
                 @pl.when(jnp.logical_and(by, z_lo == 0))
                 def _():

time: 99.8 us -> 99.9 us (level)
  no operation moved by 1% of the time
where the time goes in v4:
time: 99.9 us; the launch traced here: 99.7 us
  Pallas kernels  99.1 us (99%)
    pallas_call x1, Pallas kernels, body(): pl.pallas_call(kernel, out_shape=(jax.ShapeDtypeStruct(queries.shape, BF1...  97 us
    pallas_call x1, Pallas kernels, body(): pl.pallas_call(hand_over, out_shape=tuple((jax.ShapeDtypeStruct(a.shape,...  2.07 us

profile of v4, /device:TPU:6, one launch (start us, length us, event | category | flops | bytes accessed | tf_op | source)
XLA Modules:
  0.0 99.7 jit_solution(17628121714675090270)
XLA Ops:
  0.6 97.0 %shard_map.77 = (bf16[1,128,4096]{2,1,0:T(8,128)(2,1)}, f32[256,128]{1,0:T(8,128)}) custom-call(bf16[1,128,8192]{2,1,0:T(8,128)(2,1)} %hidden.1, bf16[1,128,4096]{2,1,0:T(8,128)(2,1)} %queries.1, bf16[1,128,512]{2,1,0:T(8,128)(2,1)} %keys.1, bf16[1,128,512]{2,1,0:T(8,128)(2,1)} %values.1, bf16[1,128,4096]{2,1,0:T(8,128)(2,1)} %out_grad.1, s32[1,128]{1,0:T(1,128)} %positions.1), custom_call_target="tpu_custom_call" | custom-call | flops 6039797760 | bytes 12582912 | tf_op jit(solution)/shard_map/pallas_call | solution.py:570
  97.7 2.1 %shard_map.78 = (bf16[1,128,4096]{2,1,0:T(8,128)(2,1)}, f32[256,128]{1,0:T(8,128)}) custom-call(bf16[1,128,4096]{2,1,0:T(8,128)(2,1)} %get-tuple-element.4.dq, f32[256,128]{1,0:T(8,128)} %get-tuple-element.5.w), custom_call_target="tpu_custom_call" | custom-call | tf_op jit(solution)/shard_map/pallas_call | solution.py:624
